TPU v7x, 256 devices: a whole 4x4x8 slice. The times are simulated.
256 devices in a mesh: tissue: 64 (over x, z, core), chan: 4 (over y).
Axes of the slice: x: 4, y: 4, z: 8, core: 2. Of those that a mesh axis runs over, the one named last changes fastest.
Arguments:
- feats: bfloat16 [768, 8192], P('chan', 'tissue'), may hold values from -6 to 6
- gate_in: bfloat16 [768, 8192], P('chan', 'tissue'), may hold values from -6 to 6
- conv_weight: float32 [9, 768], P(None, 'chan'), may hold values from -2 to 2
- conv_bias: float32 [768], P('chan'), may hold values from 0 to 2
- xproj_weight: bfloat16 [768, 320], P('chan'), may hold values from -1 to 1
- dtproj_weight: bfloat16 [4, 48, 768], P(None, None, 'chan'), may hold values from -3 to 3
- dt_bias: float32 [4, 768], P(None, 'chan'), may hold values from -6 to -2
- a_log: float32 [4, 768, 16], P(None, 'chan'), may hold values from -7 to 3
- skip_gain: float32 [4, 768], P(None, 'chan'), may hold values from 0.5 to 1.5
- row_start: int32 [64], P('tissue'), may hold values from 0 to 31
- row_len: int32 [64], P('tissue'), may hold values from 64 to 96
Outputs:
- gated_out: bfloat16 [768, 8192], P('chan', 'tissue')
Inputs may be any that keep to these rules, and one draw needn't show every extreme that they name: row_start + row_len <= 128 in every row.
All inputs are finite; a program needn't handle non-finite values.
Results may differ from a plain program's by a relative error of at most 0.0061.
Values may be sent and summed in bfloat16 or wider, within the bound.
A program may use at most 128 MiB of HBM per device.

v0:
```python
import jax
import jax.numpy as jnp
from jax import lax
from jax.experimental import pallas as pl
from jax.experimental.pallas import tpu as pltpu
from jax.sharding import PartitionSpec as P

MESH = pl.DeviceIdType.MESH
F32 = jnp.float32
BF16 = jnp.bfloat16
PEERS = 64
TEAM = 4
LEN = 128
CHAN = 192
WIDE = 256
STATE = 16
RANK = 48
GROUP = 2 * (RANK + 2 * STATE)
PACK = 2 * CHAN
STEPS = 16
LOG2E = 1.4426950408889634


def nn(a, b):
    return lax.dot_general(a, b, (((1,), (0,)), ((), ())), preferred_element_type=F32)


def nt(a, b):
    return lax.dot_general(a, b, (((1,), (1,)), ((), ())), preferred_element_type=F32)


def token_of(place):
    return lax.rem(place, 8) * STEPS + lax.div(place, 8)


def iota(shape, dim):
    return lax.broadcasted_iota(jnp.int32, shape, dim)


def one_hot(shape, equal):
    return jnp.where(equal(iota(shape, 0), iota(shape, 1)), 1.0, 0.0).astype(BF16)


def silu(v):
    return v / (1.0 + jnp.exp(-v))


def body_kernel(
    feats, gate, conv_w, conv_b, xproj, dtproj, dt_bias, a_log, skip, row_start, row_len,
    out,
    rows3, convp, xw, part, part_in, dtw, bias, decay, skips, aug,
    step, drive, proj, hexc, local, cc, carry_p,
    send_a, recv_a, send_b, recv_b, send_h, recv_h, send_c, recv_c, send_y, recv_y,
    inner_s, yrow, ycol, spare,
    ssem, rsem,
):
    me = lax.axis_index("tissue")
    team = lax.axis_index("chan")

    barrier = pltpu.get_barrier_semaphore()

    def greet(k, _):
        pl.semaphore_signal(barrier, inc=1, device_id=(lax.rem(me + k, PEERS), team), device_id_type=MESH)
        return _

    lax.fori_loop(1, PEERS, greet, 0)
    for k in range(1, TEAM):
        pl.semaphore_signal(barrier, inc=1, device_id=(me, lax.rem(team + k, TEAM)), device_id_type=MESH)

    first, width = row_start[0], row_len[0]
    cols = iota((CHAN, LEN), 1)
    lane_mask = (cols >= first) & (cols < first + width)
    rows3[:, CHAN:, :] = jnp.zeros((3, WIDE - CHAN, LEN), BF16)
    rows3[1, 0:CHAN, :] = jnp.where(lane_mask, feats[...], jnp.zeros((), BF16))

    pl.semaphore_wait(barrier, PEERS - 1 + TEAM - 1)

    below = lax.rem(me + 1, PEERS)
    above = lax.rem(me + PEERS - 1, PEERS)
    halo = [
        pltpu.make_async_remote_copy(
            src_ref=rows3.at[1, pl.ds(0, CHAN)], dst_ref=rows3.at[slot, pl.ds(0, CHAN)],
            send_sem=ssem.at[slot], recv_sem=rsem.at[slot], device_id=(peer, team), device_id_type=MESH,
        )
        for slot, peer in ((0, below), (2, above))
    ]
    for copy in halo:
        copy.start()

    shifts = one_hot((3 * LEN, LEN), lambda r, t: t == token_of(lax.rem(r, LEN)) + lax.div(r, LEN) - 1)
    convp[...] = jnp.zeros_like(convp)
    convp[0:9, 0:CHAN] = conv_w[...]
    convp[9:10, 0:CHAN] = conv_b[...]
    bias[...] = jnp.zeros_like(bias)
    bias[0:4, 0:CHAN] = dt_bias[...]
    skips[...] = jnp.zeros_like(skips)
    skips[0:1, 0:CHAN] = jnp.sum(skip[...], axis=0, keepdims=True)
    aug[...] = jnp.zeros_like(aug)

    def feature(row):
        group, f = lax.div(row, GROUP), lax.rem(row, GROUP)
        low = f < 2 * RANK
        g = f - 2 * RANK
        second = jnp.where(low, lax.div(f, RANK), lax.div(g, 2 * STATE))
        inside = jnp.where(low, lax.rem(f, RANK), RANK + lax.rem(g, 2 * STATE))
        direction = 2 * second + 1 - group
        return direction * (RANK + 2 * STATE) + inside

    order = one_hot((2 * GROUP, 2 * GROUP), lambda r, f: f == feature(r))
    xw[...] = jnp.zeros_like(xw)
    xw[:, 0:CHAN] = nt(order, xproj[...]).astype(BF16)

    dtw[...] = jnp.zeros_like(dtw)
    for d in range(4):
        pair, second = 1 - d % 2, d // 2
        dtw[pair, RANK * second : RANK * second + RANK, WIDE * second : WIDE * second + CHAN] = dtproj[d]
    decay[...] = jnp.zeros_like(decay)
    for d in range(4):
        decay[d, :, 0:CHAN] = -LOG2E * jnp.exp(a_log[d].T)

    def conv_terms(i, source):
        x = nt(shifts, source)
        total = None
        for j in range(3):
            term = convp[3 * i + j : 3 * i + j + 1, :] * x[j * LEN : (j + 1) * LEN]
            total = term if total is None else total + term
        return total

    conv_sum = convp[9:10, :] + conv_terms(1, rows3[1])
    token_rows = token_of(iota((LEN, WIDE), 0))
    row_mask = jnp.where((token_rows >= first) & (token_rows < first + width), 1.0, 0.0)

    halo[0].wait_recv()
    conv_sum = conv_sum + jnp.where(me > 0, 1.0, 0.0) * conv_terms(0, rows3[0])
    halo[1].wait_recv()
    conv_sum = conv_sum + jnp.where(me < PEERS - 1, 1.0, 0.0) * conv_terms(2, rows3[2])
    inner = (silu(conv_sum) * row_mask).astype(BF16)
    inner_s[...] = inner

    def part_copy(group, k):
        sem = 4 + 3 * group + k - 1
        return pltpu.make_async_remote_copy(
            src_ref=part.at[group], dst_ref=part_in.at[group, k - 1],
            send_sem=ssem.at[sem], recv_sem=rsem.at[sem],
            device_id=(me, lax.rem(team + k, TEAM)), device_id_type=MESH,
        )

    own = []
    for group in range(2):
        own.append(nt(xw[group * GROUP : (group + 1) * GROUP, :], inner))
        part[group] = own[group].astype(BF16)
        for k in range(1, TEAM):
            part_copy(group, k).start()

    def exchange(sem, src, dst, slot_there):
        def one(k, _):
            peer = lax.rem(me + k, PEERS)
            pltpu.make_async_remote_copy(
                src_ref=src.at[pl.ds(slot_there(me, peer)[0], 1)], dst_ref=dst.at[pl.ds(slot_there(me, peer)[1], 1)],
                send_sem=ssem.at[sem], recv_sem=rsem.at[sem], device_id=(peer, team), device_id_type=MESH,
            ).start()
            return _

        lax.fori_loop(1, PEERS, one, 0)
        here, there = slot_there(me, me)
        own_row = src.at[pl.ds(here, 1)]
        pltpu.make_async_copy(own_row, dst.at[pl.ds(there, 1)], rsem.at[sem]).start()
        pltpu.make_async_copy(own_row, spare.at[pl.ds(sem - 10, 1), pl.ds(0, src.shape[1])], ssem.at[sem]).start()

    def all_rows(sem, src, dst):
        return pltpu.make_async_remote_copy(
            src_ref=src, dst_ref=dst,
            send_sem=ssem.at[sem], recv_sem=rsem.at[sem], device_id=(below, team), device_id_type=MESH,
        )

    plain = lambda src, dst: (dst, src)

    places = [
        one_hot((WIDE, PACK), lambda e, l, b=b: (l == CHAN * b + e) & (e < CHAN)) for b in range(2)
    ]
    pick_cols = [one_hot((PEERS, LEN), lambda j, p, b=b: token_of(p) == 2 * j + b) for b in range(2)]
    put_cols = [one_hot((LEN, PEERS), lambda p, j, b=b: token_of(p) == 2 * j + b) for b in range(2)]
    pick_rows = [one_hot((PEERS, LEN), lambda r, p, b=b: token_of(p) == PEERS * b + r) for b in range(2)]
    put_rows = [one_hot((LEN, PEERS), lambda p, r, b=b: token_of(p) == PEERS * b + r) for b in range(2)]

    def pack(picked):
        return nn(picked[0].astype(BF16), places[0]) + nn(picked[1].astype(BF16), places[1])

    def unpack(message, puts):
        message = message.astype(BF16)
        return nn(puts[0], nt(message, places[0]).astype(BF16)) + nn(puts[1], nt(message, places[1]).astype(BF16))

    send_a[...] = pack([nn(pick_cols[b], inner) for b in range(2)])
    exchange(10, send_a, recv_a, plain)

    def projected(group):
        total = own[group]
        for k in range(1, TEAM):
            part_copy(group, k).wait_recv()
            total = total + part_in[group, k - 1].astype(F32)
        return total.astype(BF16)

    aug[0, 0:GROUP, :] = projected(0)
    place_lane = iota((16, LEN), 1)
    token_lane = token_of(place_lane)
    aug[0, GROUP : GROUP + 16, :] = jnp.where((token_lane >= first) & (token_lane < first + width), 1.0, 0.0).astype(BF16)
    send_b[...] = pack([nt(pick_cols[b], aug[0]) for b in range(2)])
    exchange(11, send_b, recv_b, plain)

    aug[1, 0:GROUP, :] = projected(1)
    identity = one_hot((LEN, LEN), lambda r, c: r == c)
    sub = iota((8, WIDE), 0)

    def prepare(pair, features, inner_b, mask_b):
        proj[pair] = features
        pre = nn(features[:, 0:LEN].astype(BF16), dtw[1 - pair])
        for second in range(2):
            d = 2 * second + pair
            v = pre[:, WIDE * second : WIDE * second + WIDE].astype(BF16).astype(F32) + bias[d : d + 1, :]
            size = mask_b * (jnp.maximum(v, 0.0) + jnp.log1p(jnp.exp(-jnp.abs(v))))
            step[d] = size
            drive[d] = size * inner_b

    def at(q, second):
        p = STEPS - 1 - q if second else q
        return pl.multiple_of(p * 8, 8)

    def gates(pair, second, rows):
        base = 2 * RANK + 2 * STATE * second
        tile = proj[pair, pl.ds(rows, 8), :]
        ins = [jnp.broadcast_to(tile[:, base + n : base + n + 1], (8, WIDE)) for n in range(STATE)]
        outs = [jnp.broadcast_to(tile[:, base + STATE + n : base + STATE + n + 1], (8, WIDE)) for n in range(STATE)]
        return ins, outs

    def roll_on(x, s, second, fill):
        moved = pltpu.roll(x, 8 - s if second else s, 0)
        keep = sub < 8 - s if second else sub >= s
        return jnp.where(keep, moved, fill)

    def totals(pair):
        for second in range(2):
            d = 2 * second + pair

            def advance(q, carry):
                rows = at(q, second)
                size, push = step[d, pl.ds(rows, 8), :], drive[d, pl.ds(rows, 8), :]
                ins, _ = gates(pair, second, rows)
                new = []
                for n in range(STATE):
                    now = jnp.exp2(decay[d, n : n + 1, :] * size)
                    new.append(now * carry[n] + push * ins[n])
                return tuple(new) + (carry[STATE] + size,)

            zero = jnp.zeros((8, WIDE), F32)
            ends = lax.fori_loop(0, STEPS, advance, (zero,) * (STATE + 1))
            run = ends[STATE]
            for s in (1, 2, 4):
                run = run + roll_on(run, s, second, 0.0)
            carry_p[d] = roll_on(run, 1, second, 0.0)
            end = 0 if second else 7
            for n in range(STATE):
                h, p = ends[n], jnp.exp2(decay[d, n : n + 1, :] * ends[STATE])
                for s in (1, 2, 4):
                    h = p * roll_on(h, s, second, 0.0) + h
                    if s < 4:
                        p = p * roll_on(p, s, second, 1.0)
                hexc[d, 8 * n : 8 * n + 8, :] = roll_on(h, 1, second, 0.0)
                for half in range(2):
                    k = 32 * second + 16 * half + n
                    send_h[pair, k : k + 1, 0:LEN] = h[end : end + 1, LEN * half : LEN * half + LEN]
            whole = jnp.exp2(decay[d] * run[end : end + 1, :])
            for half in range(2):
                k = 32 * second + 16 * half
                send_h[pair, k : k + STATE, LEN : 2 * LEN] = whole[:, LEN * half : LEN * half + LEN]

    def place_in_order(source, owner):
        return jnp.where(owner < PEERS // 2, source, PEERS - 1 - source)

    def send_totals(pair):
        exchange(
            12 + pair, send_h.at[pair], recv_h.at[pair], lambda src, dst: (dst, place_in_order(src, dst))
        )

    def own_scan(pair):
        all_rows(12 + pair, send_h.at[pair], recv_h.at[pair]).wait_recv()
        h, p = recv_h[pair, :, 0:LEN], recv_h[pair, :, LEN : 2 * LEN]
        row = iota((PEERS, LEN), 0)
        for s in (1, 2, 4, 8, 16, 32):
            keep = row >= s
            h = p * jnp.where(keep, pltpu.roll(h, s, 0), 0.0) + h
            if s < 32:
                p = p * jnp.where(keep, pltpu.roll(p, s, 0), 1.0)
        send_c[pair] = jnp.where(row >= 1, pltpu.roll(h, 1, 0), 0.0)
        exchange(
            14 + pair, send_c.at[pair], recv_c.at[pair], lambda src, dst: (place_in_order(dst, src), src)
        )

    def local_pass(pair):
        for second in range(2):
            d = 2 * second + pair

            def advance(q, carry):
                rows = at(q, second)
                size, push = step[d, pl.ds(rows, 8), :], drive[d, pl.ds(rows, 8), :]
                ins, outs = gates(pair, second, rows)
                since = carry[STATE] + size
                new, y = [], jnp.zeros((8, WIDE), F32)
                for n in range(STATE):
                    rate = decay[d, n : n + 1, :]
                    h = jnp.exp2(rate * size) * carry[n] + push * ins[n]
                    y = y + outs[n] * h
                    cc[d, pl.ds(rows * STATE + 8 * n, 8), :] = outs[n] * jnp.exp2(rate * since)
                    new.append(h)
                local[d, pl.ds(rows, 8), :] = y
                return tuple(new) + (since,)

            lax.fori_loop(
                0, STEPS, advance,
                tuple(hexc[d, 8 * n : 8 * n + 8, :] for n in range(STATE)) + (carry_p[d],),
            )

    def finish(pair, dst):
        all_rows(14 + pair, send_c.at[pair], recv_c.at[pair]).wait_recv()

        def advance(p, _):
            rows = pl.multiple_of(p * 8, 8)
            for half in range(2):
                lanes = slice(LEN * half, LEN * half + LEN)
                y = local[pair, pl.ds(rows, 8), lanes] + local[2 + pair, pl.ds(rows, 8), lanes]
                for second in range(2):
                    for n in range(STATE):
                        k = 32 * second + 16 * half + n
                        y = y + cc[2 * second + pair, pl.ds(rows * STATE + 8 * n, 8), lanes] * recv_c[pair, k : k + 1, :]
                dst[pl.ds(rows, 8), lanes] = y
            return _

        lax.fori_loop(0, STEPS, advance, 0)

    inner_f = inner.astype(F32)
    prepare(0, nt(identity, aug[1]), inner_f, row_mask)
    totals(0)
    send_totals(0)

    all_rows(10, send_a, recv_a).wait_recv()
    col_inner = unpack(recv_a[...], put_rows)
    all_rows(11, send_b, recv_b).wait_recv()
    col_feat = unpack(recv_b[...], put_rows)
    prepare(1, col_feat, col_inner, jnp.broadcast_to(col_feat[:, GROUP : GROUP + 1], (LEN, WIDE)))
    totals(1)
    send_totals(1)
    own_scan(0)
    local_pass(1)
    own_scan(1)
    local_pass(0)
    finish(1, ycol)
    back = ycol[...].astype(BF16)
    send_y[...] = pack([nn(pick_rows[b], back) for b in range(2)])
    exchange(16, send_y, recv_y, plain)
    finish(0, yrow)
    natural = one_hot((LEN, LEN), lambda p, t: token_of(p) == t)
    gate_rows = nt(natural, gate[...])
    gated = silu(gate_rows)
    base = yrow[:, 0:CHAN] + skips[0:1, 0:CHAN] * inner_s[:, 0:CHAN].astype(F32)
    all_rows(16, send_y, recv_y).wait_recv()
    summed = base + unpack(recv_y[...], put_cols)[:, 0:CHAN]
    result = (summed * gated).astype(BF16)
    out[...] = lax.dot_general(
        result, natural, (((0,), (0,)), ((), ())), preferred_element_type=F32
    ).astype(BF16)

    for copy in halo:
        copy.wait_send()
    for group in range(2):
        for k in range(1, TEAM):
            part_copy(group, k).wait_send()
    all_rows(10, send_a, recv_a).wait_send()
    all_rows(11, send_b, recv_b).wait_send()
    for pair in range(2):
        all_rows(12 + pair, send_h.at[pair], recv_h.at[pair]).wait_send()
        all_rows(14 + pair, send_c.at[pair], recv_c.at[pair]).wait_send()
    all_rows(16, send_y, recv_y).wait_send()


def body(
    feats, gate_in, conv_weight, conv_bias, xproj_weight, dtproj_weight, dt_bias, a_log, skip_gain, row_start, row_len
):
    vmem = pl.BlockSpec(memory_space=pltpu.VMEM)
    smem = pl.BlockSpec(memory_space=pltpu.SMEM)
    scratch = [
        ((3, WIDE, LEN), BF16),
        ((16, WIDE), F32),
        ((2 * GROUP, WIDE), BF16),
        ((2, GROUP, LEN), BF16),
        ((2, TEAM - 1, GROUP, LEN), BF16),
        ((2, LEN, 2 * WIDE), BF16),
        ((8, WIDE), F32),
        ((4, STATE, WIDE), F32),
        ((8, WIDE), F32),
        ((2, WIDE, LEN), BF16),
        ((4, LEN, WIDE), F32),
        ((4, LEN, WIDE), F32),
        ((2, LEN, WIDE), F32),
        ((4, STATE * 8, WIDE), F32),
        ((4, LEN, WIDE), F32),
        ((4, LEN * STATE, WIDE), F32),
        ((4, 8, WIDE), F32),
        ((PEERS, PACK), F32), ((PEERS, PACK), F32),
        ((PEERS, PACK), F32), ((PEERS, PACK), F32),
        ((2, PEERS, WIDE), F32), ((2, PEERS, WIDE), F32),
        ((2, PEERS, LEN), F32), ((2, PEERS, LEN), F32),
        ((PEERS, PACK), F32), ((PEERS, PACK), F32),
        ((LEN, WIDE), BF16),
        ((LEN, WIDE), F32), ((LEN, WIDE), F32),
        ((8, PACK), F32),
    ]
    return pl.pallas_call(
        body_kernel,
        out_shape=jax.ShapeDtypeStruct((CHAN, LEN), BF16),
        in_specs=[vmem] * 9 + [smem] * 2,
        out_specs=vmem,
        scratch_shapes=[pltpu.VMEM(s, t) for s, t in scratch]
        + [pltpu.SemaphoreType.DMA((17,)), pltpu.SemaphoreType.DMA((17,))],
        compiler_params=pltpu.CompilerParams(
            collective_id=0, has_side_effects=True, vmem_limit_bytes=48 * 1024 * 1024
        ),
    )(
        feats, gate_in, conv_weight, conv_bias.reshape(1, CHAN), xproj_weight, dtproj_weight, dt_bias, a_log,
        skip_gain, row_start, row_len,
    )


def solution(mesh):
    in_specs = (
        P("chan", "tissue"),
        P("chan", "tissue"),
        P(None, "chan"),
        P("chan"),
        P("chan", None),
        P(None, None, "chan"),
        P(None, "chan"),
        P(None, "chan", None),
        P(None, "chan"),
        P("tissue"),
        P("tissue"),
    )
    return jax.shard_map(body, mesh=mesh, in_specs=in_specs, out_specs=P("chan", "tissue"), check_vma=False)
```

profile of v0, /device:TPU:1, one launch (start us, length us, event | category | flops | bytes accessed | tf_op | source)
XLA Modules:
  0.0 56.8 jit_solution(11531643674675676299)
XLA Ops:
  1.3 0.0 copy-start
  1.3 0.0 copy-start.1
  1.3 0.0 copy-start.2
  1.3 0.0 copy-start.3
  1.3 0.0 copy-start.4
  1.3 0.0 copy-start.5
  1.4 0.0 copy-start.6
  1.4 0.0 copy-start.7
  1.4 1.2 %copy.12.a_log = f32[4,192,16]{2,1,0:T(8,128)S(1)} copy(f32[4,192,16]{1,2,0:T(8,128)} %param.18) | data formatting | bytes 98304 | tf_op args[7]
  2.5 0.0 copy-done
  2.6 0.0 copy-done.1
  2.6 0.0 copy-done.2
  2.6 0.0 copy-done.3
  2.6 0.0 copy-done.4
  2.6 0.0 copy-done.5
  2.6 0.0 copy-done.6
  2.6 0.0 copy-done.7
  2.6 53.6 %shard_map.109 = bf16[192,128]{1,0:T(8,128)(2,1)S(1)} custom-call(bf16[192,128]{1,0:T(8,128)(2,1)S(1)} %copy-done.2, bf16[192,128]{1,0:T(8,128)(2,1)S(1)} %copy-done.3, f32[9,192]{1,0:T(8,128)S(1)} %copy-done.4, f32[1,192]{1,0:T(1,128)S(1)} %bitcast.1, bf16[192,320]{1,0:T(8,128)(2,1)S(1)} %copy-done, bf16[4,48,192]{2,1,0:T(8,128)(2,1)S(1)} %copy-done.1, ...), custom_call_target="tpu_custom_call" | custom-call | tf_op jit(solution)/shard_map/pallas_call | solution.py:416
  56.2 0.6 %copy.16 = bf16[192,128]{1,0:T(8,128)(2,1)} copy(bf16[192,128]{1,0:T(8,128)(2,1)S(1)} %shard_map.109) | data formatting | bytes 98304
Async XLA Ops:
  1.3 1.3 %copy-start = (bf16[192,320]{1,0:T(8,128)(2,1)S(1)}, bf16[192,320]{1,0:T(8,128)(2,1)}, u32[]{:S(2)}) copy-start(bf16[192,320]{1,0:T(8,128)(2,1)} %xproj.1) | copy-start | bytes 368644
  1.3 1.3 %copy-start.1 = (bf16[4,48,192]{2,1,0:T(8,128)(2,1)S(1)}, bf16[4,48,192]{2,1,0:T(8,128)(2,1)}, u32[]{:S(2)}) copy-start(bf16[4,48,192]{2,1,0:T(8,128)(2,1)} %dtproj.1) | copy-start | bytes 221188
  1.3 1.3 %copy-start.2 = (bf16[192,128]{1,0:T(8,128)(2,1)S(1)}, bf16[192,128]{1,0:T(8,128)(2,1)}, u32[]{:S(2)}) copy-start(bf16[192,128]{1,0:T(8,128)(2,1)} %feats.1) | copy-start | bytes 147460
  1.3 1.3 %copy-start.3 = (bf16[192,128]{1,0:T(8,128)(2,1)S(1)}, bf16[192,128]{1,0:T(8,128)(2,1)}, u32[]{:S(2)}) copy-start(bf16[192,128]{1,0:T(8,128)(2,1)} %gate.1) | copy-start | bytes 147460
  1.3 1.3 %copy-start.4 = (f32[9,192]{1,0:T(8,128)S(1)}, f32[9,192]{1,0:T(8,128)}, u32[]{:S(2)}) copy-start(f32[9,192]{1,0:T(8,128)} %conv_w.1) | copy-start | bytes 20740
  1.3 1.3 %copy-start.5 = (f32[4,192]{1,0:T(4,128)S(1)}, f32[4,192]{1,0:T(4,128)}, u32[]{:S(2)}) copy-start(f32[4,192]{1,0:T(4,128)} %dt_bias.1) | copy-start | bytes 9220
  1.4 1.3 %copy-start.6 = (f32[4,192]{1,0:T(4,128)S(1)}, f32[4,192]{1,0:T(4,128)}, u32[]{:S(2)}) copy-start(f32[4,192]{1,0:T(4,128)} %skip.1) | copy-start | bytes 9220
  1.4 1.3 %copy-start.7 = (f32[192]{0:T(256)S(1)}, f32[192]{0:T(256)}, u32[]{:S(2)}) copy-start(f32[192]{0:T(256)} %param.14) | copy-start | bytes 2308
where the time goes:
time: 56.9 us; the launch traced here: 56.8 us
  Pallas kernels  53.6 us (94%)
  local copies, waits for them, and re-layouts  1.82 us (3%)
  between operations  1.44 us (3%)
    pallas_call x1, Pallas kernels, body(): pl.pallas_call(body_kernel, out_shape=jax.ShapeDtypeStruct((CHAN, LEN), B...  53.6 us
    unnamed x18, local copies, waits for them, and re-layouts  1.82 us

commit v1 on v0

--- a/solution.py
+++ b/solution.py
@@ -29,8 +29,12 @@
     return lax.dot_general(a, b, (((1,), (1,)), ((), ())), preferred_element_type=F32)
 
 
+def tn(a, b):
+    return lax.dot_general(a, b, (((0,), (0,)), ((), ())), preferred_element_type=F32)
+
+
 def token_of(place):
-    return lax.rem(place, 8) * STEPS + lax.div(place, 8)
+    return (place & 7) * STEPS + (place >> 3)
 
 
 def iota(shape, dim):
@@ -46,13 +50,14 @@
 
 
 def body_kernel(
+    feats_hbm, gate_hbm, conv_w_hbm, conv_b_hbm, xproj_hbm, dtproj_hbm, dt_bias_hbm, a_log_hbm, skip_hbm, start_hbm, len_hbm,
+    out,
     feats, gate, conv_w, conv_b, xproj, dtproj, dt_bias, a_log, skip, row_start, row_len,
-    out,
     rows3, convp, xw, part, part_in, dtw, bias, decay, skips, aug,
     step, drive, proj, hexc, local, cc, carry_p,
     send_a, recv_a, send_b, recv_b, send_h, recv_h, send_c, recv_c, send_y, recv_y,
     inner_s, yrow, ycol, spare,
-    ssem, rsem,
+    ssem, rsem, isem,
 ):
     me = lax.axis_index("tissue")
     team = lax.axis_index("chan")
@@ -67,11 +72,50 @@
     for k in range(1, TEAM):
         pl.semaphore_signal(barrier, inc=1, device_id=(me, lax.rem(team + k, TEAM)), device_id_type=MESH)
 
+    loads = [
+        pltpu.make_async_copy(src, dst, isem.at[n])
+        for n, (src, dst) in enumerate((
+            (start_hbm, row_start), (len_hbm, row_len), (feats_hbm, feats), (xproj_hbm, xproj), (conv_w_hbm, conv_w),
+            (conv_b_hbm, conv_b), (dtproj_hbm, dtproj), (dt_bias_hbm, dt_bias), (a_log_hbm, a_log), (skip_hbm, skip),
+            (gate_hbm, gate),
+        ))
+    ]
+    for load in loads:
+        load.start()
+    rows3[:, CHAN:, :] = jnp.zeros((3, WIDE - CHAN, LEN), BF16)
+    for load in loads:
+        load.wait()
+
     first, width = row_start[0], row_len[0]
     cols = iota((CHAN, LEN), 1)
     lane_mask = (cols >= first) & (cols < first + width)
-    rows3[:, CHAN:, :] = jnp.zeros((3, WIDE - CHAN, LEN), BF16)
     rows3[1, 0:CHAN, :] = jnp.where(lane_mask, feats[...], jnp.zeros((), BF16))
+
+    shifts = one_hot((3 * LEN, LEN), lambda r, t: t == token_of(r & (LEN - 1)) + (r >> 7) - 1)
+    convp[...] = jnp.zeros_like(convp)
+    convp[0:9, 0:CHAN] = conv_w[...]
+    convp[9:10, 0:CHAN] = conv_b[...]
+    bias[...] = jnp.zeros_like(bias)
+    bias[0:4, 0:CHAN] = dt_bias[...]
+    skips[...] = jnp.zeros_like(skips)
+    skips[0:1, 0:CHAN] = jnp.sum(skip[...], axis=0, keepdims=True)
+    aug[...] = jnp.zeros_like(aug)
+
+    turned = nt(one_hot((2 * GROUP, 2 * GROUP), lambda r, f: r == f), xproj[...]).astype(BF16)
+    xw[...] = jnp.zeros_like(xw)
+    for d in range(4):
+        top, start = GROUP * (1 - d % 2), (RANK + 2 * STATE) * d
+        low, gat = top + RANK * (d // 2), top + 2 * RANK + 2 * STATE * (d // 2)
+        xw[low : low + RANK, 0:CHAN] = turned[start : start + RANK]
+        xw[gat : gat + 2 * STATE, 0:CHAN] = turned[start + RANK : start + RANK + 2 * STATE]
+
+    dtw[...] = jnp.zeros_like(dtw)
+    for d in range(4):
+        pair, second = 1 - d % 2, d // 2
+        dtw[pair, RANK * second : RANK * second + RANK, WIDE * second : WIDE * second + CHAN] = dtproj[d]
+    decay[...] = jnp.zeros_like(decay)
+    for d in range(4):
+        decay[d, :, 0:CHAN] = -LOG2E * jnp.exp(a_log[d])
 
     pl.semaphore_wait(barrier, PEERS - 1 + TEAM - 1)
 
@@ -87,37 +131,6 @@
     for copy in halo:
         copy.start()
 
-    shifts = one_hot((3 * LEN, LEN), lambda r, t: t == token_of(lax.rem(r, LEN)) + lax.div(r, LEN) - 1)
-    convp[...] = jnp.zeros_like(convp)
-    convp[0:9, 0:CHAN] = conv_w[...]
-    convp[9:10, 0:CHAN] = conv_b[...]
-    bias[...] = jnp.zeros_like(bias)
-    bias[0:4, 0:CHAN] = dt_bias[...]
-    skips[...] = jnp.zeros_like(skips)
-    skips[0:1, 0:CHAN] = jnp.sum(skip[...], axis=0, keepdims=True)
-    aug[...] = jnp.zeros_like(aug)
-
-    def feature(row):
-        group, f = lax.div(row, GROUP), lax.rem(row, GROUP)
-        low = f < 2 * RANK
-        g = f - 2 * RANK
-        second = jnp.where(low, lax.div(f, RANK), lax.div(g, 2 * STATE))
-        inside = jnp.where(low, lax.rem(f, RANK), RANK + lax.rem(g, 2 * STATE))
-        direction = 2 * second + 1 - group
-        return direction * (RANK + 2 * STATE) + inside
-
-    order = one_hot((2 * GROUP, 2 * GROUP), lambda r, f: f == feature(r))
-    xw[...] = jnp.zeros_like(xw)
-    xw[:, 0:CHAN] = nt(order, xproj[...]).astype(BF16)
-
-    dtw[...] = jnp.zeros_like(dtw)
-    for d in range(4):
-        pair, second = 1 - d % 2, d // 2
-        dtw[pair, RANK * second : RANK * second + RANK, WIDE * second : WIDE * second + CHAN] = dtproj[d]
-    decay[...] = jnp.zeros_like(decay)
-    for d in range(4):
-        decay[d, :, 0:CHAN] = -LOG2E * jnp.exp(a_log[d].T)
-
     def conv_terms(i, source):
         x = nt(shifts, source)
         total = None
@@ -166,6 +179,14 @@
         own_row = src.at[pl.ds(here, 1)]
         pltpu.make_async_copy(own_row, dst.at[pl.ds(there, 1)], rsem.at[sem]).start()
         pltpu.make_async_copy(own_row, spare.at[pl.ds(sem - 10, 1), pl.ds(0, src.shape[1])], ssem.at[sem]).start()
+        due[sem] = all_rows(sem, src, dst)
+        sent.append(due[sem])
+
+    def arrive(sem):
+        due.pop(sem).wait_recv()
+
+    sent = list(halo)
+    due = {}
 
     def all_rows(sem, src, dst):
         return pltpu.make_async_remote_copy(
@@ -238,28 +259,40 @@
         return jnp.where(keep, moved, fill)
 
     def totals(pair):
+        part_states = STATE // 2
+        zero = jnp.zeros((8, WIDE), F32)
+        ends = {}
+        for base in range(0, STATE, part_states):
+
+            def advance(q, carry):
+                new = []
+                for second in range(2):
+                    d, rows = 2 * second + pair, at(q, second)
+                    size, push = step[d, pl.ds(rows, 8), :], drive[d, pl.ds(rows, 8), :]
+                    tile = proj[pair, pl.ds(rows, 8), :]
+                    lane = 2 * RANK + 2 * STATE * second + base
+                    for n in range(part_states):
+                        now = jnp.exp2(decay[d, base + n : base + n + 1, :] * size)
+                        gate_in = jnp.broadcast_to(tile[:, lane + n : lane + n + 1], (8, WIDE))
+                        new.append(now * carry[part_states * second + n] + push * gate_in)
+                return tuple(new)
+
+            got = lax.fori_loop(0, STEPS, advance, (zero,) * (2 * part_states), unroll=4)
+            for second in range(2):
+                for n in range(part_states):
+                    ends[second, base + n] = got[part_states * second + n]
         for second in range(2):
             d = 2 * second + pair
-
-            def advance(q, carry):
-                rows = at(q, second)
-                size, push = step[d, pl.ds(rows, 8), :], drive[d, pl.ds(rows, 8), :]
-                ins, _ = gates(pair, second, rows)
-                new = []
-                for n in range(STATE):
-                    now = jnp.exp2(decay[d, n : n + 1, :] * size)
-                    new.append(now * carry[n] + push * ins[n])
-                return tuple(new) + (carry[STATE] + size,)
-
-            zero = jnp.zeros((8, WIDE), F32)
-            ends = lax.fori_loop(0, STEPS, advance, (zero,) * (STATE + 1))
-            run = ends[STATE]
+            chunk = step[d, 0:8, :]
+            for q in range(1, STEPS):
+                chunk = chunk + step[d, 8 * q : 8 * q + 8, :]
+            run = chunk
             for s in (1, 2, 4):
                 run = run + roll_on(run, s, second, 0.0)
             carry_p[d] = roll_on(run, 1, second, 0.0)
             end = 0 if second else 7
             for n in range(STATE):
-                h, p = ends[n], jnp.exp2(decay[d, n : n + 1, :] * ends[STATE])
+                h, p = ends[second, n], jnp.exp2(decay[d, n : n + 1, :] * chunk)
                 for s in (1, 2, 4):
                     h = p * roll_on(h, s, second, 0.0) + h
                     if s < 4:
@@ -282,7 +315,7 @@
         )
 
     def own_scan(pair):
-        all_rows(12 + pair, send_h.at[pair], recv_h.at[pair]).wait_recv()
+        arrive(12 + pair)
         h, p = recv_h[pair, :, 0:LEN], recv_h[pair, :, LEN : 2 * LEN]
         row = iota((PEERS, LEN), 0)
         for s in (1, 2, 4, 8, 16, 32):
@@ -320,7 +353,7 @@
             )
 
     def finish(pair, dst):
-        all_rows(14 + pair, send_c.at[pair], recv_c.at[pair]).wait_recv()
+        arrive(14 + pair)
 
         def advance(p, _):
             rows = pl.multiple_of(p * 8, 8)
@@ -341,9 +374,9 @@
     totals(0)
     send_totals(0)
 
-    all_rows(10, send_a, recv_a).wait_recv()
+    arrive(10)
     col_inner = unpack(recv_a[...], put_rows)
-    all_rows(11, send_b, recv_b).wait_recv()
+    arrive(11)
     col_feat = unpack(recv_b[...], put_rows)
     prepare(1, col_feat, col_inner, jnp.broadcast_to(col_feat[:, GROUP : GROUP + 1], (LEN, WIDE)))
     totals(1)
@@ -358,34 +391,32 @@
     exchange(16, send_y, recv_y, plain)
     finish(0, yrow)
     natural = one_hot((LEN, LEN), lambda p, t: token_of(p) == t)
-    gate_rows = nt(natural, gate[...])
-    gated = silu(gate_rows)
-    base = yrow[:, 0:CHAN] + skips[0:1, 0:CHAN] * inner_s[:, 0:CHAN].astype(F32)
-    all_rows(16, send_y, recv_y).wait_recv()
-    summed = base + unpack(recv_y[...], put_cols)[:, 0:CHAN]
-    result = (summed * gated).astype(BF16)
-    out[...] = lax.dot_general(
-        result, natural, (((0,), (0,)), ((), ())), preferred_element_type=F32
-    ).astype(BF16)
-
-    for copy in halo:
+    base = yrow[...] + skips[0:1, :] * inner_s[...].astype(F32)
+    high = base.astype(BF16)
+    base = (tn(high, natural) + tn((base - high.astype(F32)).astype(BF16), natural))[0:CHAN]
+    gated = silu(gate[...].astype(F32))
+    arrive(16)
+    back = recv_y[...].astype(BF16)
+    spots = [one_hot((PEERS, LEN), lambda j, t, b=b: t == 2 * j + b) for b in range(2)]
+    returned = tn(back, spots[0])[0:CHAN] + tn(back, spots[1])[CHAN:PACK]
+    out[...] = ((base + returned) * gated).astype(BF16)
+
+    for copy in sent:
         copy.wait_send()
     for group in range(2):
         for k in range(1, TEAM):
             part_copy(group, k).wait_send()
-    all_rows(10, send_a, recv_a).wait_send()
-    all_rows(11, send_b, recv_b).wait_send()
-    for pair in range(2):
-        all_rows(12 + pair, send_h.at[pair], recv_h.at[pair]).wait_send()
-        all_rows(14 + pair, send_c.at[pair], recv_c.at[pair]).wait_send()
-    all_rows(16, send_y, recv_y).wait_send()
 
 
 def body(
     feats, gate_in, conv_weight, conv_bias, xproj_weight, dtproj_weight, dt_bias, a_log, skip_gain, row_start, row_len
 ):
     vmem = pl.BlockSpec(memory_space=pltpu.VMEM)
-    smem = pl.BlockSpec(memory_space=pltpu.SMEM)
+    hbm = pl.BlockSpec(memory_space=pltpu.HBM)
+    inputs = [
+        ((CHAN, LEN), BF16), ((CHAN, LEN), BF16), ((9, CHAN), F32), ((1, CHAN), F32), ((CHAN, 2 * GROUP), BF16),
+        ((4, RANK, CHAN), BF16), ((4, CHAN), F32), ((4, STATE, CHAN), F32), ((4, CHAN), F32),
+    ]
     scratch = [
         ((3, WIDE, LEN), BF16),
         ((16, WIDE), F32),
@@ -416,16 +447,17 @@
     return pl.pallas_call(
         body_kernel,
         out_shape=jax.ShapeDtypeStruct((CHAN, LEN), BF16),
-        in_specs=[vmem] * 9 + [smem] * 2,
+        in_specs=[hbm] * 11,
         out_specs=vmem,
-        scratch_shapes=[pltpu.VMEM(s, t) for s, t in scratch]
-        + [pltpu.SemaphoreType.DMA((17,)), pltpu.SemaphoreType.DMA((17,))],
+        scratch_shapes=[pltpu.VMEM(s, t) for s, t in inputs] + [pltpu.SMEM((1,), jnp.int32)] * 2
+        + [pltpu.VMEM(s, t) for s, t in scratch]
+        + [pltpu.SemaphoreType.DMA((17,)), pltpu.SemaphoreType.DMA((17,)), pltpu.SemaphoreType.DMA((11,))],
         compiler_params=pltpu.CompilerParams(
-            collective_id=0, has_side_effects=True, vmem_limit_bytes=48 * 1024 * 1024
+            collective_id=0, has_side_effects=True, vmem_limit_bytes=56 * 1024 * 1024
         ),
     )(
-        feats, gate_in, conv_weight, conv_bias.reshape(1, CHAN), xproj_weight, dtproj_weight, dt_bias, a_log,
-        skip_gain, row_start, row_len,
+        feats, gate_in, conv_weight, conv_bias.reshape(1, CHAN), xproj_weight, dtproj_weight, dt_bias,
+        jnp.swapaxes(a_log, 1, 2), skip_gain, row_start, row_len,
     )
 
 

time: 56.9 us -> 55.3 us (0.972)
  Pallas kernels: 53.6 us -> 52.4 us
    pallas_call x1, Pallas kernels: 53.6 us -> 52.4 us  [body(): pl.pallas_call(body_kernel, out_shape=jax.ShapeDtypeStruct((CHAN, LEN), B...]
    unnamed x18 -> x1, local copies, waits for them, and re-layouts: 1.82 us -> 1.42 us
where the time goes in v1:
time: 55.3 us; the launch traced here: 55.1 us
  Pallas kernels  52.4 us (95%)
  local copies, waits for them, and re-layouts  1.42 us (3%)
  between operations  1.3 us (2%)
    pallas_call x1, Pallas kernels, body(): pl.pallas_call(body_kernel, out_shape=jax.ShapeDtypeStruct((CHAN, LEN), B...  52.4 us
    unnamed x1, local copies, waits for them, and re-layouts  1.42 us

profile of v1, /device:TPU:1, one launch (start us, length us, event | category | flops | bytes accessed | tf_op | source)
XLA Modules:
  0.0 55.1 jit_solution(127425280196753247)
XLA Ops:
  1.3 52.4 %shard_map.109 = bf16[192,128]{1,0:T(8,128)(2,1)} custom-call(bf16[192,128]{1,0:T(8,128)(2,1)} %feats_hbm.1, bf16[192,128]{1,0:T(8,128)(2,1)} %gate_hbm.1, f32[9,192]{1,0:T(8,128)} %conv_w_hbm.1, f32[1,192]{1,0:T(1,128)} %bitcast.3, bf16[192,320]{1,0:T(8,128)(2,1)} %xproj_hbm.1, bf16[4,48,192]{2,1,0:T(8,128)(2,1)} %dtproj_hbm.1, f32[4,192]{1,0:T(4,128)} %dt_bias_hbm.1, ...), custom_call_target="tpu_custom_call" | custom-call | tf_op jit(solution)/shard_map/pallas_call | solution.py:447
  53.7 1.4 %copy.15 = bf16[192,128]{1,0:T(8,128)(2,1)} copy(bf16[192,128]{1,0:T(8,128)(2,1)} %shard_map.109) | data formatting | bytes 98304

commit v2 on v1

--- a/solution.py
+++ b/solution.py
@@ -64,12 +64,18 @@
 
     barrier = pltpu.get_barrier_semaphore()
 
-    def greet(k, _):
-        pl.semaphore_signal(barrier, inc=1, device_id=(lax.rem(me + k, PEERS), team), device_id_type=MESH)
+    def away(i):
+        q, j = i >> 4, (i >> 1) & 7
+        dx = 2 + (q >> 1) - (q & 1) * (1 + 2 * (q >> 1))
+        dz = 4 + (j >> 1) - (j & 1) * (1 + 2 * (j >> 1))
+        return (((me >> 4) + dx) & 3) * 16 + (((me >> 1) + dz) & 7) * 2 + ((me + i + 1) & 1)
+
+    def greet(i, _):
+        pl.semaphore_signal(barrier, inc=1, device_id=(away(i), team), device_id_type=MESH)
         return _
 
-    lax.fori_loop(1, PEERS, greet, 0)
-    for k in range(1, TEAM):
+    lax.fori_loop(0, PEERS - 1, greet, 0)
+    for k in (2, 1, 3):
         pl.semaphore_signal(barrier, inc=1, device_id=(me, lax.rem(team + k, TEAM)), device_id_type=MESH)
 
     loads = [
@@ -86,7 +92,7 @@
     for load in loads:
         load.wait()
 
-    first, width = row_start[0], row_len[0]
+    first, width = row_start[0, 0], row_len[0, 0]
     cols = iota((CHAN, LEN), 1)
     lane_mask = (cols >= first) & (cols < first + width)
     rows3[1, 0:CHAN, :] = jnp.where(lane_mask, feats[...], jnp.zeros((), BF16))
@@ -162,19 +168,19 @@
     for group in range(2):
         own.append(nt(xw[group * GROUP : (group + 1) * GROUP, :], inner))
         part[group] = own[group].astype(BF16)
-        for k in range(1, TEAM):
+        for k in (2, 1, 3):
             part_copy(group, k).start()
 
     def exchange(sem, src, dst, slot_there):
-        def one(k, _):
-            peer = lax.rem(me + k, PEERS)
+        def one(i, _):
+            peer = away(i)
             pltpu.make_async_remote_copy(
                 src_ref=src.at[pl.ds(slot_there(me, peer)[0], 1)], dst_ref=dst.at[pl.ds(slot_there(me, peer)[1], 1)],
                 send_sem=ssem.at[sem], recv_sem=rsem.at[sem], device_id=(peer, team), device_id_type=MESH,
             ).start()
             return _
 
-        lax.fori_loop(1, PEERS, one, 0)
+        lax.fori_loop(0, PEERS - 1, one, 0)
         here, there = slot_there(me, me)
         own_row = src.at[pl.ds(here, 1)]
         pltpu.make_async_copy(own_row, dst.at[pl.ds(there, 1)], rsem.at[sem]).start()
@@ -359,15 +365,17 @@
             rows = pl.multiple_of(p * 8, 8)
             for half in range(2):
                 lanes = slice(LEN * half, LEN * half + LEN)
-                y = local[pair, pl.ds(rows, 8), lanes] + local[2 + pair, pl.ds(rows, 8), lanes]
-                for second in range(2):
-                    for n in range(STATE):
+                sums = [local[pair, pl.ds(rows, 8), lanes], local[2 + pair, pl.ds(rows, 8), lanes], None, None]
+                for n in range(STATE):
+                    for second in range(2):
                         k = 32 * second + 16 * half + n
-                        y = y + cc[2 * second + pair, pl.ds(rows * STATE + 8 * n, 8), lanes] * recv_c[pair, k : k + 1, :]
-                dst[pl.ds(rows, 8), lanes] = y
+                        term = cc[2 * second + pair, pl.ds(rows * STATE + 8 * n, 8), lanes] * recv_c[pair, k : k + 1, :]
+                        spot = (2 * n + second) % 4
+                        sums[spot] = term if sums[spot] is None else sums[spot] + term
+                dst[pl.ds(rows, 8), lanes] = (sums[0] + sums[1]) + (sums[2] + sums[3])
             return _
 
-        lax.fori_loop(0, STEPS, advance, 0)
+        lax.fori_loop(0, STEPS, advance, 0, unroll=4)
 
     inner_f = inner.astype(F32)
     prepare(0, nt(identity, aug[1]), inner_f, row_mask)
@@ -449,7 +457,7 @@
         out_shape=jax.ShapeDtypeStruct((CHAN, LEN), BF16),
         in_specs=[hbm] * 11,
         out_specs=vmem,
-        scratch_shapes=[pltpu.VMEM(s, t) for s, t in inputs] + [pltpu.SMEM((1,), jnp.int32)] * 2
+        scratch_shapes=[pltpu.VMEM(s, t) for s, t in inputs] + [pltpu.SMEM((1, 1), jnp.int32)] * 2
         + [pltpu.VMEM(s, t) for s, t in scratch]
         + [pltpu.SemaphoreType.DMA((17,)), pltpu.SemaphoreType.DMA((17,)), pltpu.SemaphoreType.DMA((11,))],
         compiler_params=pltpu.CompilerParams(
@@ -457,7 +465,7 @@
         ),
     )(
         feats, gate_in, conv_weight, conv_bias.reshape(1, CHAN), xproj_weight, dtproj_weight, dt_bias,
-        jnp.swapaxes(a_log, 1, 2), skip_gain, row_start, row_len,
+        jnp.swapaxes(a_log, 1, 2), skip_gain, row_start.reshape(1, 1), row_len.reshape(1, 1),
     )
 
 

time: 55.3 us -> 52.7 us (0.953)
  Pallas kernels: 52.4 us -> 49.8 us
    pallas_call x1, Pallas kernels: 52.4 us -> 49.8 us  [body(): pl.pallas_call(body_kernel, out_shape=jax.ShapeDtypeStruct((CHAN, LEN), B...]
where the time goes in v2:
time: 52.7 us; the launch traced here: 52.5 us
  Pallas kernels  49.8 us (94%)
  local copies, waits for them, and re-layouts  1.42 us (3%)
  between operations  1.3 us (2%)
    pallas_call x1, Pallas kernels, body(): pl.pallas_call(body_kernel, out_shape=jax.ShapeDtypeStruct((CHAN, LEN), B...  49.8 us
    unnamed x1, local copies, waits for them, and re-layouts  1.42 us

profile of v2, /device:TPU:1, one launch (start us, length us, event | category | flops | bytes accessed | tf_op | source)
XLA Modules:
  0.0 52.5 jit_solution(4462831587265073163)
XLA Ops:
  1.3 49.8 %shard_map.109 = bf16[192,128]{1,0:T(8,128)(2,1)} custom-call(bf16[192,128]{1,0:T(8,128)(2,1)} %feats_hbm.1, bf16[192,128]{1,0:T(8,128)(2,1)} %gate_hbm.1, f32[9,192]{1,0:T(8,128)} %conv_w_hbm.1, f32[1,192]{1,0:T(1,128)} %bitcast.7, bf16[192,320]{1,0:T(8,128)(2,1)} %xproj_hbm.1, bf16[4,48,192]{2,1,0:T(8,128)(2,1)} %dtproj_hbm.1, f32[4,192]{1,0:T(4,128)} %dt_bias_hbm.1, ...), custom_call_target="tpu_custom_call" | custom-call | tf_op jit(solution)/shard_map/pallas_call | solution.py:455
  51.1 1.4 %copy.15 = bf16[192,128]{1,0:T(8,128)(2,1)} copy(bf16[192,128]{1,0:T(8,128)(2,1)} %shard_map.109) | data formatting | bytes 98304

commit v3 on v2

--- a/solution.py
+++ b/solution.py
@@ -64,17 +64,24 @@
 
     barrier = pltpu.get_barrier_semaphore()
 
-    def away(i):
-        q, j = i >> 4, (i >> 1) & 7
-        dx = 2 + (q >> 1) - (q & 1) * (1 + 2 * (q >> 1))
-        dz = 4 + (j >> 1) - (j & 1) * (1 + 2 * (j >> 1))
-        return (((me >> 4) + dx) & 3) * 16 + (((me >> 1) + dz) & 7) * 2 + ((me + i + 1) & 1)
-
-    def greet(i, _):
-        pl.semaphore_signal(barrier, inc=1, device_id=(away(i), team), device_id_type=MESH)
-        return _
-
-    lax.fori_loop(0, PEERS - 1, greet, 0)
+    plane, core = me >> 4, me & 1
+    lines = [(((me >> 1) + dz) & 7) * 2 for dz in (4, 3, 5, 2, 6, 1, 7, 0)]
+
+    def to_peers(act):
+        def one(q, _):
+            base = ((plane + 2 + (q >> 1) - (q & 1)) & 3) * 16
+            for line in lines:
+                for other in (1 - core, core):
+                    act(base + line + other)
+            return _
+
+        lax.fori_loop(0, 3, one, 0)
+        for line in lines:
+            act(plane * 16 + line + 1 - core)
+        for line in lines[:-1]:
+            act(plane * 16 + line + core)
+
+    to_peers(lambda peer: pl.semaphore_signal(barrier, inc=1, device_id=(peer, team), device_id_type=MESH))
     for k in (2, 1, 3):
         pl.semaphore_signal(barrier, inc=1, device_id=(me, lax.rem(team + k, TEAM)), device_id_type=MESH)
 
@@ -172,15 +179,14 @@
             part_copy(group, k).start()
 
     def exchange(sem, src, dst, slot_there):
-        def one(i, _):
-            peer = away(i)
+        def send(peer):
+            here, there = slot_there(me, peer)
             pltpu.make_async_remote_copy(
-                src_ref=src.at[pl.ds(slot_there(me, peer)[0], 1)], dst_ref=dst.at[pl.ds(slot_there(me, peer)[1], 1)],
+                src_ref=src.at[pl.ds(here, 1)], dst_ref=dst.at[pl.ds(there, 1)],
                 send_sem=ssem.at[sem], recv_sem=rsem.at[sem], device_id=(peer, team), device_id_type=MESH,
             ).start()
-            return _
-
-        lax.fori_loop(0, PEERS - 1, one, 0)
+
+        to_peers(send)
         here, there = slot_there(me, me)
         own_row = src.at[pl.ds(here, 1)]
         pltpu.make_async_copy(own_row, dst.at[pl.ds(there, 1)], rsem.at[sem]).start()
@@ -389,9 +395,9 @@
     prepare(1, col_feat, col_inner, jnp.broadcast_to(col_feat[:, GROUP : GROUP + 1], (LEN, WIDE)))
     totals(1)
     send_totals(1)
-    own_scan(0)
     local_pass(1)
     own_scan(1)
+    own_scan(0)
     local_pass(0)
     finish(1, ycol)
     back = ycol[...].astype(BF16)

time: 52.7 us -> 52 us (0.987)
  Pallas kernels: 49.8 us -> 49.1 us
    pallas_call x1, Pallas kernels: 49.8 us -> 49.1 us  [body(): pl.pallas_call(body_kernel, out_shape=jax.ShapeDtypeStruct((CHAN, LEN), B...]
where the time goes in v3:
time: 52 us; the launch traced here: 51.8 us
  Pallas kernels  49.1 us (94%)
  local copies, waits for them, and re-layouts  1.42 us (3%)
  between operations  1.3 us (2%)
    pallas_call x1, Pallas kernels, body(): pl.pallas_call(body_kernel, out_shape=jax.ShapeDtypeStruct((CHAN, LEN), B...  49.1 us
    unnamed x1, local copies, waits for them, and re-layouts  1.42 us

profile of v3, /device:TPU:1, one launch (start us, length us, event | category | flops | bytes accessed | tf_op | source)
XLA Modules:
  0.0 51.8 jit_solution(15724474603296329286)
XLA Ops:
  1.3 49.1 %shard_map.109 = bf16[192,128]{1,0:T(8,128)(2,1)} custom-call(bf16[192,128]{1,0:T(8,128)(2,1)} %feats_hbm.1, bf16[192,128]{1,0:T(8,128)(2,1)} %gate_hbm.1, f32[9,192]{1,0:T(8,128)} %conv_w_hbm.1, f32[1,192]{1,0:T(1,128)} %bitcast.7, bf16[192,320]{1,0:T(8,128)(2,1)} %xproj_hbm.1, bf16[4,48,192]{2,1,0:T(8,128)(2,1)} %dtproj_hbm.1, f32[4,192]{1,0:T(4,128)} %dt_bias_hbm.1, ...), custom_call_target="tpu_custom_call" | custom-call | tf_op jit(solution)/shard_map/pallas_call | solution.py:461
  50.4 1.4 %copy.15 = bf16[192,128]{1,0:T(8,128)(2,1)} copy(bf16[192,128]{1,0:T(8,128)(2,1)} %shard_map.109) | data formatting | bytes 98304

commit v4 on v3

--- a/solution.py
+++ b/solution.py
@@ -208,22 +208,22 @@
 
     plain = lambda src, dst: (dst, src)
 
-    places = [
-        one_hot((WIDE, PACK), lambda e, l, b=b: (l == CHAN * b + e) & (e < CHAN)) for b in range(2)
-    ]
-    pick_cols = [one_hot((PEERS, LEN), lambda j, p, b=b: token_of(p) == 2 * j + b) for b in range(2)]
-    put_cols = [one_hot((LEN, PEERS), lambda p, j, b=b: token_of(p) == 2 * j + b) for b in range(2)]
-    pick_rows = [one_hot((PEERS, LEN), lambda r, p, b=b: token_of(p) == PEERS * b + r) for b in range(2)]
-    put_rows = [one_hot((LEN, PEERS), lambda p, r, b=b: token_of(p) == PEERS * b + r) for b in range(2)]
+    places = one_hot(
+        (2 * WIDE, PACK), lambda e, l: (l == CHAN * (e >> 8) + (e & (WIDE - 1))) & ((e & (WIDE - 1)) < CHAN)
+    )
+    pick_cols = one_hot((LEN, LEN), lambda m, p: token_of(p) == 2 * (m & (PEERS - 1)) + (m >> 6))
+    pick_rows = one_hot((LEN, LEN), lambda m, p: token_of(p) == m)
+    put_rows = one_hot((LEN, LEN), lambda p, m: token_of(p) == m)
 
     def pack(picked):
-        return nn(picked[0].astype(BF16), places[0]) + nn(picked[1].astype(BF16), places[1])
+        picked = picked.astype(BF16)
+        return nn(picked[0:PEERS], places[0:WIDE]) + nn(picked[PEERS:], places[WIDE:])
 
     def unpack(message, puts):
-        message = message.astype(BF16)
-        return nn(puts[0], nt(message, places[0]).astype(BF16)) + nn(puts[1], nt(message, places[1]).astype(BF16))
-
-    send_a[...] = pack([nn(pick_cols[b], inner) for b in range(2)])
+        apart = nt(message.astype(BF16), places).astype(BF16)
+        return nn(puts, jnp.concatenate([apart[:, 0:WIDE], apart[:, WIDE:]], axis=0))
+
+    send_a[...] = pack(nn(pick_cols, inner))
     exchange(10, send_a, recv_a, plain)
 
     def projected(group):
@@ -237,7 +237,7 @@
     place_lane = iota((16, LEN), 1)
     token_lane = token_of(place_lane)
     aug[0, GROUP : GROUP + 16, :] = jnp.where((token_lane >= first) & (token_lane < first + width), 1.0, 0.0).astype(BF16)
-    send_b[...] = pack([nt(pick_cols[b], aug[0]) for b in range(2)])
+    send_b[...] = pack(nt(pick_cols, aug[0]))
     exchange(11, send_b, recv_b, plain)
 
     aug[1, 0:GROUP, :] = projected(1)
@@ -289,7 +289,7 @@
                         new.append(now * carry[part_states * second + n] + push * gate_in)
                 return tuple(new)
 
-            got = lax.fori_loop(0, STEPS, advance, (zero,) * (2 * part_states), unroll=4)
+            got = lax.fori_loop(0, STEPS, advance, (zero,) * (2 * part_states), unroll=16)
             for second in range(2):
                 for n in range(part_states):
                     ends[second, base + n] = got[part_states * second + n]
@@ -381,7 +381,7 @@
                 dst[pl.ds(rows, 8), lanes] = (sums[0] + sums[1]) + (sums[2] + sums[3])
             return _
 
-        lax.fori_loop(0, STEPS, advance, 0, unroll=4)
+        lax.fori_loop(0, STEPS, advance, 0, unroll=8)
 
     inner_f = inner.astype(F32)
     prepare(0, nt(identity, aug[1]), inner_f, row_mask)
@@ -401,7 +401,7 @@
     local_pass(0)
     finish(1, ycol)
     back = ycol[...].astype(BF16)
-    send_y[...] = pack([nn(pick_rows[b], back) for b in range(2)])
+    send_y[...] = pack(nn(pick_rows, back))
     exchange(16, send_y, recv_y, plain)
     finish(0, yrow)
     natural = one_hot((LEN, LEN), lambda p, t: token_of(p) == t)
@@ -409,10 +409,11 @@
     high = base.astype(BF16)
     base = (tn(high, natural) + tn((base - high.astype(F32)).astype(BF16), natural))[0:CHAN]
     gated = silu(gate[...].astype(F32))
+    spots = one_hot((PEERS, 2 * LEN), lambda j, m: (m & (LEN - 1)) == 2 * j + (m >> 7))
     arrive(16)
     back = recv_y[...].astype(BF16)
-    spots = [one_hot((PEERS, LEN), lambda j, t, b=b: t == 2 * j + b) for b in range(2)]
-    returned = tn(back, spots[0])[0:CHAN] + tn(back, spots[1])[CHAN:PACK]
+    spread = tn(back, spots)
+    returned = spread[0:CHAN, 0:LEN] + spread[CHAN:PACK, LEN : 2 * LEN]
     out[...] = ((base + returned) * gated).astype(BF16)
 
     for copy in sent:
@@ -460,7 +461,7 @@
     ]
     return pl.pallas_call(
         body_kernel,
-        out_shape=jax.ShapeDtypeStruct((CHAN, LEN), BF16),
+        out_shape=pltpu.VMEM((CHAN, LEN), BF16),
         in_specs=[hbm] * 11,
         out_specs=vmem,
         scratch_shapes=[pltpu.VMEM(s, t) for s, t in inputs] + [pltpu.SMEM((1, 1), jnp.int32)] * 2

time: 52 us -> 50.3 us (0.967)
  Pallas kernels: 49.1 us -> 48.3 us
  local copies, waits for them, and re-layouts: 1.42 us -> 0.62 us
    pallas_call x1, Pallas kernels: 49.1 us -> 48.3 us  [body(): pl.pallas_call(body_kernel, out_shape=pltpu.VMEM((CHAN, LEN), BF16), in_s...]
    unnamed x1, local copies, waits for them, and re-layouts: 1.42 us -> 0.62 us
where the time goes in v4:
time: 50.3 us; the launch traced here: 50.2 us
  Pallas kernels  48.3 us (96%)
  between operations  1.3 us (3%)
  local copies, waits for them, and re-layouts  0.62 us (1%)
    pallas_call x1, Pallas kernels, body(): pl.pallas_call(body_kernel, out_shape=pltpu.VMEM((CHAN, LEN), BF16), in_s...  48.3 us

profile of v4, /device:TPU:1, one launch (start us, length us, event | category | flops | bytes accessed | tf_op | source)
XLA Modules:
  0.0 50.2 jit_solution(10982297550169554270)
XLA Ops:
  1.3 48.3 %shard_map.109 = bf16[192,128]{1,0:T(8,128)(2,1)S(1)} custom-call(bf16[192,128]{1,0:T(8,128)(2,1)} %feats_hbm.1, bf16[192,128]{1,0:T(8,128)(2,1)} %gate_hbm.1, f32[9,192]{1,0:T(8,128)} %conv_w_hbm.1, f32[1,192]{1,0:T(1,128)} %bitcast.7, bf16[192,320]{1,0:T(8,128)(2,1)} %xproj_hbm.1, bf16[4,48,192]{2,1,0:T(8,128)(2,1)} %dtproj_hbm.1, f32[4,192]{1,0:T(4,128)} %dt_bias_hbm.1, ...), custom_call_target="tpu_custom_call" | custom-call | tf_op jit(solution)/shard_map/pallas_call | solution.py:462
  49.6 0.6 %copy.13 = bf16[192,128]{1,0:T(8,128)(2,1)} copy(bf16[192,128]{1,0:T(8,128)(2,1)S(1)} %shard_map.109) | data formatting | bytes 98304

commit v5 on v4

--- a/solution.py
+++ b/solution.py
@@ -172,11 +172,14 @@
         )
 
     own = []
-    for group in range(2):
+
+    def send_part(group):
         own.append(nt(xw[group * GROUP : (group + 1) * GROUP, :], inner))
         part[group] = own[group].astype(BF16)
         for k in (2, 1, 3):
             part_copy(group, k).start()
+
+    send_part(0)
 
     def exchange(sem, src, dst, slot_there):
         def send(peer):
@@ -239,6 +242,7 @@
     aug[0, GROUP : GROUP + 16, :] = jnp.where((token_lane >= first) & (token_lane < first + width), 1.0, 0.0).astype(BF16)
     send_b[...] = pack(nt(pick_cols, aug[0]))
     exchange(11, send_b, recv_b, plain)
+    send_part(1)
 
     aug[1, 0:GROUP, :] = projected(1)
     identity = one_hot((LEN, LEN), lambda r, c: r == c)

time: 50.3 us -> 49.7 us (0.988)
  Pallas kernels: 48.3 us -> 47.6 us
    pallas_call x1, Pallas kernels: 48.3 us -> 47.6 us  [body(): pl.pallas_call(body_kernel, out_shape=pltpu.VMEM((CHAN, LEN), BF16), in_s...]
where the time goes in v5:
time: 49.7 us; the launch traced here: 49.5 us
  Pallas kernels  47.6 us (96%)
  between operations  1.3 us (3%)
  local copies, waits for them, and re-layouts  0.62 us (1%)
    pallas_call x1, Pallas kernels, body(): pl.pallas_call(body_kernel, out_shape=pltpu.VMEM((CHAN, LEN), BF16), in_s...  47.6 us

profile of v5, /device:TPU:1, one launch (start us, length us, event | category | flops | bytes accessed | tf_op | source)
XLA Modules:
  0.0 49.5 jit_solution(7173561420935861052)
XLA Ops:
  1.3 47.6 %shard_map.109 = bf16[192,128]{1,0:T(8,128)(2,1)S(1)} custom-call(bf16[192,128]{1,0:T(8,128)(2,1)} %feats_hbm.1, bf16[192,128]{1,0:T(8,128)(2,1)} %gate_hbm.1, f32[9,192]{1,0:T(8,128)} %conv_w_hbm.1, f32[1,192]{1,0:T(1,128)} %bitcast.7, bf16[192,320]{1,0:T(8,128)(2,1)} %xproj_hbm.1, bf16[4,48,192]{2,1,0:T(8,128)(2,1)} %dtproj_hbm.1, f32[4,192]{1,0:T(4,128)} %dt_bias_hbm.1, ...), custom_call_target="tpu_custom_call" | custom-call | tf_op jit(solution)/shard_map/pallas_call | solution.py:466
  48.9 0.6 %copy.13 = bf16[192,128]{1,0:T(8,128)(2,1)} copy(bf16[192,128]{1,0:T(8,128)(2,1)S(1)} %shard_map.109) | data formatting | bytes 98304

commit v6 on v5

--- a/solution.py
+++ b/solution.py
@@ -244,7 +244,6 @@
     exchange(11, send_b, recv_b, plain)
     send_part(1)
 
-    aug[1, 0:GROUP, :] = projected(1)
     identity = one_hot((LEN, LEN), lambda r, c: r == c)
     sub = iota((8, WIDE), 0)
 
@@ -344,8 +343,8 @@
             14 + pair, send_c.at[pair], recv_c.at[pair], lambda src, dst: (place_in_order(dst, src), src)
         )
 
-    def local_pass(pair):
-        for second in range(2):
+    def local_pass(pair, seconds=(0, 1)):
+        for second in seconds:
             d = 2 * second + pair
 
             def advance(q, carry):
@@ -388,9 +387,6 @@
         lax.fori_loop(0, STEPS, advance, 0, unroll=8)
 
     inner_f = inner.astype(F32)
-    prepare(0, nt(identity, aug[1]), inner_f, row_mask)
-    totals(0)
-    send_totals(0)
 
     arrive(10)
     col_inner = unpack(recv_a[...], put_rows)
@@ -399,14 +395,19 @@
     prepare(1, col_feat, col_inner, jnp.broadcast_to(col_feat[:, GROUP : GROUP + 1], (LEN, WIDE)))
     totals(1)
     send_totals(1)
-    local_pass(1)
+    aug[1, 0:GROUP, :] = projected(1)
+    prepare(0, nt(identity, aug[1]), inner_f, row_mask)
+    totals(0)
+    send_totals(0)
+    local_pass(1, (0,))
     own_scan(1)
+    local_pass(1, (1,))
     own_scan(0)
-    local_pass(0)
     finish(1, ycol)
     back = ycol[...].astype(BF16)
     send_y[...] = pack(nn(pick_rows, back))
     exchange(16, send_y, recv_y, plain)
+    local_pass(0)
     finish(0, yrow)
     natural = one_hot((LEN, LEN), lambda p, t: token_of(p) == t)
     base = yrow[...] + skips[0:1, :] * inner_s[...].astype(F32)

time: 49.7 us -> 49.2 us (0.990)
  no operation moved by 1% of the time
where the time goes in v6:
time: 49.2 us; the launch traced here: 49.1 us
  Pallas kernels  47.2 us (96%)
  between operations  1.3 us (3%)
  local copies, waits for them, and re-layouts  0.62 us (1%)
    pallas_call x1, Pallas kernels, body(): pl.pallas_call(body_kernel, out_shape=pltpu.VMEM((CHAN, LEN), BF16), in_s...  47.2 us

profile of v6, /device:TPU:1, one launch (start us, length us, event | category | flops | bytes accessed | tf_op | source)
XLA Modules:
  0.0 49.1 jit_solution(6564096790620963917)
XLA Ops:
  1.3 47.2 %shard_map.109 = bf16[192,128]{1,0:T(8,128)(2,1)S(1)} custom-call(bf16[192,128]{1,0:T(8,128)(2,1)} %feats_hbm.1, bf16[192,128]{1,0:T(8,128)(2,1)} %gate_hbm.1, f32[9,192]{1,0:T(8,128)} %conv_w_hbm.1, f32[1,192]{1,0:T(1,128)} %bitcast.7, bf16[192,320]{1,0:T(8,128)(2,1)} %xproj_hbm.1, bf16[4,48,192]{2,1,0:T(8,128)(2,1)} %dtproj_hbm.1, f32[4,192]{1,0:T(4,128)} %dt_bias_hbm.1, ...), custom_call_target="tpu_custom_call" | custom-call | tf_op jit(solution)/shard_map/pallas_call | solution.py:467
  48.5 0.6 %copy.13 = bf16[192,128]{1,0:T(8,128)(2,1)} copy(bf16[192,128]{1,0:T(8,128)(2,1)S(1)} %shard_map.109) | data formatting | bytes 98304
